TPU v7x, 32 devices: a whole 2x2x4 slice. The times are simulated.
32 devices in a mesh: tp: 2 (over core), dp: 16 (over z, y, x).
Axes of the slice: x: 2, y: 2, z: 4, core: 2. Of those that a mesh axis runs over, the one named last changes fastest.
Arguments:
- hidden: bfloat16 [32768, 8192], P('dp', 'tp')
- norm_gain: bfloat16 [8192], P('tp'), may hold values from 0.099609375 to 1.8984375
- projection: bfloat16 [8192, 1024], P('tp'), may hold values from -0.0625 to 0.0625
- centroids: bfloat16 [65536, 1024], P('dp'), may hold values from -6 to 6
- owners: int32 [32768, 1], P(('dp', 'tp')), may hold values from 0 to 15; in each aligned block of 1024 rows (0 to 1023, 1024 to 2047, ...) at most 192 rows name the same one
- local_list: int32 [32768], P(('dp', 'tp')), may hold values from 0 to 4095
- slot_table: int32 [32, 3072], P(('dp', 'tp')), may hold values from 0 to 3071, each once within a row
Outputs:
- codes: bfloat16 [98304, 1024], P(('dp', 'tp'))
Inputs may be any that keep to these rules, and one draw needn't show every extreme that they name: `owners`: in the 1024 tokens of one device no owner is named more than 192 times; some device names an owner exactly 192 times. `slot_table`: each row is a permutation of 0 to 3071.
All inputs are finite; a program needn't handle non-finite values.
Results may differ from a plain program's by a relative error of at most 0.011.
Values may be sent and summed in bfloat16 or wider, within the bound.
No kernel may reach another device: no remote copies, remote signals or barrier semaphores. Data moves between devices by JAX's collectives and lax.ppermute only.
A program may use at most 128 MiB of HBM per device.

v0:
```python
import functools

import jax
import jax.numpy as jnp
from jax import lax
from jax.experimental import pallas as pl
from jax.experimental.pallas import tpu as pltpu
from jax.sharding import PartitionSpec as P

D = 8192
EPSILON = 1e-05
LANES = 128
MIB = 1024 * 1024
PLANES = 4
FAR_STRIDE = 4096
HIDDEN = pl.CostEstimate(flops=1, bytes_accessed=1, transcendentals=0)
F32 = jnp.float32
BF16 = jnp.bfloat16
I32 = jnp.int32


def iota(shape, dim):
    return lax.broadcasted_iota(I32, shape, dim)


def fit(total, wanted):
    best = 16
    for size in range(16, min(total, wanted) + 1, 16):
        if total % size == 0:
            best = size
    return best


def params(mib):
    return pltpu.CompilerParams(vmem_limit_bytes=mib * MIB)


def partial_kernel(which, hidden, gain, projection, out, total, squares):
    step = pl.program_id(0)
    rows, depth = hidden.shape
    tile = fit(rows, 512)

    @pl.when(step == 0)
    def _():
        total[...] = jnp.zeros_like(total)
        squares[...] = jnp.zeros_like(squares)

    @pl.loop(0, rows // tile)
    def _(i):
        at = pl.ds(pl.multiple_of(i * tile, tile), tile)
        block = hidden[at, :]
        total[at, :] += jnp.dot(block * gain[...], projection[...], preferred_element_type=F32)
        wide = block.astype(F32)
        wide = wide * wide
        part = wide[:, :LANES]
        for lane in range(LANES, depth, LANES):
            part = part + wide[:, lane : lane + LANES]
        squares[at, :] += part

    @pl.when(step == pl.num_programs(0) - 1)
    def _():
        width = total.shape[1]

        @pl.loop(0, rows // tile)
        def _(i):
            at = pl.ds(pl.multiple_of(i * tile, tile), tile)
            out[at, :width] = total[at, :].astype(BF16)
            energy = squares[at, :]
            high = energy.astype(BF16)
            wide = high.astype(F32)
            out[at, width : width + LANES] = high
            out[at, width + LANES :] = jnp.where(wide < 3e38, energy - wide, 0.0).astype(BF16)


def partial_keys(which, hidden, gain, projection, rows):
    depth, width = projection.shape
    block = 1024
    return pl.pallas_call(
        partial_kernel,
        grid_spec=pltpu.PrefetchScalarGridSpec(
            num_scalar_prefetch=1,
            grid=(depth // block,),
            in_specs=[
                pl.BlockSpec((rows, block), lambda k, w: (w[0], k)),
                pl.BlockSpec((1, block), lambda k, w: (0, k)),
                pl.BlockSpec((block, width), lambda k, w: (k, 0)),
            ],
            out_specs=pl.BlockSpec((rows, width + 2 * LANES), lambda k, w: (0, 0)),
            scratch_shapes=[pltpu.VMEM((rows, width), F32), pltpu.VMEM((rows, LANES), F32)],
        ),
        out_shape=jax.ShapeDtypeStruct((rows, width + 2 * LANES), BF16),
        compiler_params=params(60),
        cost_estimate=pl.CostEstimate(
            flops=2 * rows * depth * width,
            bytes_accessed=2 * (rows * depth + depth * width + rows * width),
            transcendentals=0,
        ),
        name="partial_keys",
    )(which, hidden, gain, projection)


def route_kernel(plan, me, owners, lists, place, sent):
    n_dp, cap = plan.n_dp, plan.cap
    size = plan.plane
    rows = owners.shape[1]
    n_own = plan.n_own
    wide = plan.wide
    plane = me[0] // size
    hot = iota((n_own, rows), 0) == owners[...]
    onehot = hot.astype(F32).astype(BF16)
    before = (iota((rows, rows), 0) < iota((rows, rows), 1)).astype(F32).astype(BF16)
    ranks = jnp.dot(onehot, before, preferred_element_type=F32)

    def of_token(column):
        return jnp.sum(jnp.where(hot, column, 0.0), axis=0, keepdims=True)

    def bits(owner):
        return jnp.where(owner < n_dp, (owner // size) ^ plane, PLANES)

    def counts(mask):
        return lax.dot_general(
            mask.astype(F32).astype(BF16), onehot, (((1,), (1,)), ((), ())), preferred_element_type=F32
        )[0:1, :]

    def column(mask):
        return jnp.sum(jnp.where(hot & mask, 1.0, 0.0), axis=1, keepdims=True)

    token = iota((1, rows), 1)
    early = token < plan.early
    direct_row = jnp.minimum(counts(iota((8, rows), 1) < plan.early), float(plan.direct))
    direct_col = jnp.minimum(column(early), float(plan.direct))
    all_row = counts(iota((8, rows), 1) >= 0) - direct_row
    all_col = column(token >= 0) - direct_col
    bits_row = bits(iota((1, n_own), 1))
    bits_col = bits(iota((n_own, 1), 0))

    level = iota((n_own, wide), 1).astype(F32)

    def wave(col, row, near_cap):
        out_col = jnp.where(bits_col == 0, jnp.minimum(col, near_cap), col)
        out_row = jnp.where(bits_row == 0, jnp.minimum(row, near_cap), row)
        for e in range(1, PLANES):
            mine = bits_col == e
            filled = jnp.sum(jnp.where(mine, jnp.minimum(col, level), 0.0), axis=0, keepdims=True)
            fits = (filled <= float(plan.far)) & (level[0:1, :] <= float(plan.each))
            limit = jnp.sum(jnp.where(fits, 1.0, 0.0), axis=1, keepdims=True) - 1.0
            out_col = jnp.where(mine, jnp.minimum(col, limit), out_col)
            out_row = jnp.where(bits_row == e, jnp.minimum(row, limit), out_row)
        return out_col, out_row

    half_col = jnp.where(bits_col == 0, all_col, jnp.floor((all_col + 1.0) * 0.5))
    half_row = jnp.where(bits_row == 0, all_row, jnp.floor((all_row + 1.0) * 0.5))
    first_col, first_row = wave(half_col, half_row, float(plan.near_cap))
    second_col, second_row = wave(all_col - first_col, all_row - first_row, 0.0)
    third_row = all_row - first_row - second_row

    def starts(row):
        ahead = (iota((n_own, n_own), 1) < iota((n_own, n_own), 0)) & (bits_row == bits_col)
        return jnp.sum(jnp.where(ahead, row, 0.0), axis=1, keepdims=True)

    by_rank = of_token(ranks)
    straight = early & (by_rank < of_token(direct_col))
    rank = by_rank - of_token(direct_col)
    first_n = of_token(first_col)
    second_n = of_token(second_col)
    e_token = (owners[...] // size) ^ plane
    in_first = ~straight & (rank < first_n)
    in_third = ~straight & (rank >= first_n + second_n)
    in_second = ~(straight | in_first | in_third)
    stride = (e_token - 1) * FAR_STRIDE
    first_at = stride + (of_token(starts(first_row)) + rank).astype(I32)
    second_at = stride + (of_token(starts(second_row)) + rank - first_n).astype(I32)
    third_at = owners[...] * cap + (rank - first_n - second_n).astype(I32)
    near_at = ((owners[...] % size) ^ (me[0] % size)) * plan.near_cap + rank.astype(I32)
    place[...] = jnp.full(place.shape, -1, I32)
    place[0:1, :] = jnp.where(in_first & (e_token > 0), first_at, -1)
    place[1:2, :] = jnp.where(in_first & (e_token == 0), near_at, -1)
    place[2:3, :] = jnp.where(in_second, second_at, -1)
    place[3:4, :] = jnp.where(straight, owners[...] * plan.direct + by_rank.astype(I32), -1)
    place[4:5, :] = jnp.where(in_third, third_at, -1)

    at_rank = (iota((wide, rows), 0).astype(F32) == by_rank).astype(F32).astype(BF16)
    high = (lists[...] // 64).astype(F32)
    low = (lists[...] % 64).astype(F32)

    def by_owner(values):
        picked = jnp.where(hot, values, 0.0).astype(BF16)
        return lax.dot_general(picked, at_rank, (((1,), (1,)), ((), ())), preferred_element_type=F32)

    live = by_owner(jnp.ones_like(high))
    ids = by_owner(high) * 64.0 + by_owner(low)
    step = jnp.max(third_row, axis=1, keepdims=True)
    for base in range(0, 2 * plan.sent, plan.sent):
        sent[:, base : base + wide] = jnp.where(live > 0.5, ids, -1.0).astype(I32)[:n_dp, :]
        start = base + wide
        for row in (direct_row, first_row, second_row):
            sent[:, start : start + n_own] = jnp.broadcast_to(row.astype(I32), (n_dp, n_own))
            start += n_own
        sent[:, start : start + LANES] = jnp.broadcast_to(step.astype(I32), (n_dp, LANES))


def route(plan, me, owners, lists):
    rows = owners.shape[1]
    return pl.pallas_call(
        functools.partial(route_kernel, plan),
        grid_spec=pltpu.PrefetchScalarGridSpec(
            num_scalar_prefetch=1,
            grid=(1,),
            in_specs=[pl.BlockSpec((1, rows), lambda i, m: (0, 0))] * 2,
            out_specs=(
                pl.BlockSpec((8, rows), lambda i, m: (0, 0)),
                pl.BlockSpec((plan.n_dp, 2 * plan.sent), lambda i, m: (0, 0)),
            ),
        ),
        out_shape=(
            jax.ShapeDtypeStruct((8, rows), I32),
            jax.ShapeDtypeStruct((plan.n_dp, 2 * plan.sent), I32),
        ),
        compiler_params=params(32),
        cost_estimate=pl.CostEstimate(
            flops=2 * rows * rows * plan.n_own, bytes_accessed=rows * 64, transcendentals=0
        ),
        name="route",
    )(me, owners, lists)


def slot_kernel(plan, me, heard, table, direct, near, first, second, third, counts):
    size = plan.plane
    wide, n_own = plan.wide, plan.n_own
    plane = me[0] // size
    owner = iota((plan.n_dp, n_own), 1)

    def listed(wave):
        return heard[:, wide + wave * n_own : wide + (wave + 1) * n_own]

    def mine(wave):
        return jnp.sum(jnp.where(owner == me[0], listed(wave), 0), axis=1, keepdims=True)

    def skip(slots, count):
        shift = 1
        while shift < wide:
            moved = pltpu.roll(slots, wide - shift, 1)
            slots = jnp.where((count // shift) % 2 == 1, moved, slots)
            shift *= 2
        return slots

    def of_bits(values, e):
        picked = jnp.zeros((size, values.shape[1]), I32)
        for q in range(PLANES):
            picked = jnp.where((plane ^ e) == q, values[q * size : (q + 1) * size, :], picked)
        return picked

    def by_distance(part, i):
        picked = iota((size, 1), 0) == ((me[0] % size) ^ i)
        return jnp.sum(jnp.where(picked, part, 0), axis=0, keepdims=True)

    n_direct, n_first, n_second = mine(0), mine(1), mine(2)
    total = jnp.sum(jnp.where(heard[:, :wide] >= 0, 1, 0), axis=1, keepdims=True)
    lane = iota((plan.n_dp, wide), 1)
    slots = table[...]
    direct[...] = jnp.where(lane < n_direct, slots, -1)
    slots = skip(slots, n_direct)
    in_first = jnp.where(lane < n_first, slots, -1)
    slots = skip(slots, n_first)
    in_second = jnp.where(lane < n_second, slots, -1)
    slots = skip(slots, n_second)
    third[...] = jnp.where(lane < total - n_direct - n_first - n_second, slots, -1)
    for i in range(size):
        near[i : i + 1, :] = by_distance(of_bits(in_first, 0), i)
    source = iota((plan.n_dp, 1), 0)
    for wave, values, out in ((0, in_first, first), (1, in_second, second)):
        for e in range(1, PLANES):
            part = of_bits(values, e)
            for i in range(size):
                at = i * (PLANES - 1) + e - 1
                out[at : at + 1, :] = by_distance(part, i)
            from_me = source == (plane ^ e) * size + me[0] % size
            at = wave * 4 + e - 1
            counts[at : at + 1, :] = jnp.sum(
                jnp.where(from_me, listed(1 + wave), 0), axis=0, keepdims=True
            )


def wave_slots(plan, me, heard, table):
    size = plan.plane
    shapes = [
        (plan.n_dp, plan.wide),
        (size, plan.wide),
        (size * (PLANES - 1), plan.wide),
        (size * (PLANES - 1), plan.wide),
        (plan.n_dp, plan.wide),
        (8, plan.n_own),
    ]
    return pl.pallas_call(
        functools.partial(slot_kernel, plan),
        grid_spec=pltpu.PrefetchScalarGridSpec(
            num_scalar_prefetch=1,
            grid=(1,),
            in_specs=[
                pl.BlockSpec((plan.n_dp, plan.sent), lambda i, m: (0, 0)),
                pl.BlockSpec((plan.n_dp, plan.wide), lambda i, m: (0, 0)),
            ],
            out_specs=tuple(pl.BlockSpec(shape, lambda i, m: (0, 0)) for shape in shapes),
        ),
        out_shape=tuple(jax.ShapeDtypeStruct(shape, I32) for shape in shapes),
        compiler_params=params(32),
        cost_estimate=HIDDEN,
        name="wave_slots",
    )(me, heard, table)


def combine(own, other, keys):
    rows, width = keys.shape
    tile = fit(rows, 128)

    @pl.loop(0, rows // tile)
    def _(i):
        at = pl.ds(pl.multiple_of(i * tile, tile), tile)
        parts = own[at, width:].astype(F32) + other[at, width:].astype(F32)
        energy = jnp.sum(parts, axis=1, keepdims=True)
        scale = lax.rsqrt(energy * (1.0 / D) + EPSILON)
        terms = own[at, :width].astype(F32) + other[at, :width].astype(F32)
        keys[at, :] = jnp.where(scale > 0.0, terms * scale, 0.0).astype(BF16)


def permute(line, first, place, chunks, out):
    total = None
    start = 0
    for keys in chunks:
        rows = keys.shape[0]
        places = place[line : line + 1, start : start + rows]
        start += rows
        onehot = (iota((out.shape[0], rows), 0) + first == places).astype(F32).astype(BF16)
        part = jnp.dot(onehot, keys[...], preferred_element_type=F32)
        total = part if total is None else total + part
    out[...] = total.astype(BF16)


def pack_kernel(moves, n_keys, fresh, place, *refs):
    chunks = refs[:n_keys]
    if fresh:
        own, other = refs[n_keys : n_keys + 2]
        outs, keys = refs[n_keys + 2 : -1], refs[-1]
        combine(own, other, keys)
        chunks = (*chunks, keys)
    else:
        outs = refs[n_keys:]
    for (line, first, _), out in zip(moves, outs):
        permute(line, first, place, chunks, out)


def pack(moves, place, keys, fresh=()):
    width = keys[0].shape[1] if keys else fresh[0].shape[1] - 2 * LANES
    sizes = [size for _, _, size in moves] + [part.shape[0] for part in fresh[:1]]
    rows = place.shape[1]
    whole = lambda i: (0, 0)
    operands = [place, *keys, *fresh]
    return list(
        pl.pallas_call(
            functools.partial(pack_kernel, moves, len(keys), bool(fresh)),
            grid=(1,),
            in_specs=[pl.BlockSpec(part.shape, whole) for part in operands],
            out_specs=tuple(pl.BlockSpec((size, width), whole) for size in sizes),
            out_shape=tuple(jax.ShapeDtypeStruct((size, width), BF16) for size in sizes),
            compiler_params=params(60),
            cost_estimate=HIDDEN,
            name="pack_keys",
        )(*operands)
    )


def spread_kernel(plan, wave, me, counts, *refs):
    size = plan.plane
    outs = refs[len(refs) - size :]
    refs = refs[: len(refs) - size]
    cap = plan.each
    base = (me[0] // size) * size
    for e in range(1, PLANES):
        rows = refs[e - 1]
        row = iota((cap, rows.shape[0]), 0)
        column = iota(row.shape, 1)
        at = wave * 4 + e - 1
        hits = []
        for k in range(size):
            owner = (me[0] % size) ^ k
            start = lax.fori_loop(0, owner, lambda i, total: total + counts[at, base + i], 0)
            hit = (column == row + start) & (row < counts[at, base + owner])
            hits.append(hit.astype(F32).astype(BF16))
        moved = jnp.dot(
            jnp.concatenate(hits, axis=0), rows[...], preferred_element_type=F32
        ).astype(BF16)
        for k in range(size):
            outs[k][(e - 1) * cap : e * cap, :] = moved[k * cap : (k + 1) * cap, :]


def spread(plan, wave, me, counts, packed):
    width = packed[0].shape[1]
    each = (PLANES - 1) * plan.each
    whole = lambda i, m, c: (0, 0)
    return list(
        pl.pallas_call(
            functools.partial(spread_kernel, plan, wave),
            grid_spec=pltpu.PrefetchScalarGridSpec(
                num_scalar_prefetch=2,
                grid=(1,),
                in_specs=[pl.BlockSpec(block.shape, whole) for block in packed],
                out_specs=(pl.BlockSpec((each, width), whole),) * plan.plane,
            ),
            out_shape=(jax.ShapeDtypeStruct((each, width), BF16),) * plan.plane,
            compiler_params=params(60),
            cost_estimate=HIDDEN,
            name="spread_rows",
        )(me, counts, *packed)
    )


def centre_kernel(n_in, slots, lists, centroids, out, table, placed):
    step = pl.program_id(0)
    block = centroids.shape[0]
    n_lists = n_in * block
    chunks = centroids.shape[1] // LANES
    count = placed.shape[0] // chunks
    size = out.shape[0]

    @pl.when(step == 0)
    def _():
        table[pl.ds(n_lists * chunks, chunks), :] = jnp.zeros((chunks, LANES), F32)

    @pl.when(step < n_in)
    def _():
        @pl.loop(0, block // 16)
        def _(i):
            wide = centroids[pl.ds(pl.multiple_of(i * 16, 16), 16), :].astype(F32)
            for top in range(0, 16, 8):
                first = (step * block + i * 16 + top) * chunks
                for c in range(chunks):
                    part = wide[top : top + 8, c * LANES : (c + 1) * LANES]
                    table[pl.ds(first + c, 8, stride=chunks), :] = part

    @pl.when(step == n_in)
    def _():
        @pl.loop(0, count // 16)
        def _(i):
            found = []
            for u in range(16):
                a = i * 16 + u
                row = table[pl.ds(pl.multiple_of(lists[a], chunks), chunks), :]
                found.append((slots[a], row))
            for at, row in found:
                placed[pl.ds(pl.multiple_of(at, chunks), chunks), :] = -row

    @pl.when(step >= n_in)
    def _():
        @pl.loop(0, size // 16)
        def _(i):
            rows = []
            for top in range(0, 16, 8):
                first = ((step - n_in) * size + i * 16 + top) * chunks
                rows.append(
                    jnp.concatenate(
                        [placed[pl.ds(first + c, 8, stride=chunks), :] for c in range(chunks)], axis=1
                    )
                )
            out[pl.ds(pl.multiple_of(i * 16, 16), 16), :] = jnp.concatenate(rows, axis=0).astype(BF16)


def centres(slots, lists, centroids):
    count = slots.shape[0]
    n_lists, width = centroids.shape
    slots = slots * (width // LANES)
    lists = jnp.where(lists < 0, n_lists, lists) * (width // LANES)
    block, size = fit(n_lists, 512), fit(count, 512)
    n_in = n_lists // block
    chunks = width // LANES
    return pl.pallas_call(
        functools.partial(centre_kernel, n_in),
        grid_spec=pltpu.PrefetchScalarGridSpec(
            num_scalar_prefetch=2,
            grid=(n_in + count // size,),
            in_specs=[pl.BlockSpec((block, width), lambda i, s, l: (jnp.minimum(i, n_in - 1), 0))],
            out_specs=pl.BlockSpec((size, width), lambda i, s, l: (jnp.maximum(i - n_in, 0), 0)),
            scratch_shapes=[
                pltpu.VMEM(((n_lists + 1) * chunks, LANES), F32),
                pltpu.VMEM((count * chunks, LANES), F32),
            ],
        ),
        out_shape=jax.ShapeDtypeStruct((count, width), BF16),
        compiler_params=params(60),
        cost_estimate=HIDDEN,
        name="centroid_rows",
    )(slots, lists, centroids)


def place_kernel(sizes, slots, before, *refs):
    parts, out, arrived, sems = refs[: len(sizes)], *refs[len(sizes) :]
    tile = out.shape[0]
    step = pl.program_id(0)
    first = step * tile

    @pl.when(step == 0)
    def _():
        copies = []
        start = 0
        for i, (part, size) in enumerate(zip(parts, sizes)):
            copies.append(pltpu.make_async_copy(part, arrived.at[pl.ds(start, size)], sems.at[i]))
            start += size
        for copy in copies:
            copy.start()
        for copy in copies:
            copy.wait()

    onehot = (slots[...] == iota((tile, slots.shape[1]), 0) + first).astype(F32).astype(BF16)
    keys = jnp.dot(onehot, arrived[...], preferred_element_type=F32)
    out[...] = (keys + before[...].astype(F32)).astype(BF16)


def place_rows(slots, arrived, before):
    count, width = before.shape
    sizes = [part.shape[0] for part in arrived]
    n_rows = sum(sizes)
    tile = fit(count, 512)
    return pl.pallas_call(
        functools.partial(place_kernel, sizes),
        grid=(count // tile,),
        in_specs=[
            pl.BlockSpec((1, n_rows), lambda i: (0, 0)),
            pl.BlockSpec((tile, width), lambda i: (i, 0)),
        ]
        + [pl.BlockSpec(memory_space=pl.ANY)] * len(sizes),
        out_specs=pl.BlockSpec((tile, width), lambda i: (i, 0)),
        out_shape=jax.ShapeDtypeStruct((count, width), BF16),
        scratch_shapes=[
            pltpu.VMEM((n_rows, width), BF16),
            pltpu.SemaphoreType.DMA((len(sizes),)),
        ],
        compiler_params=params(60),
        cost_estimate=HIDDEN,
        name="residual_rows",
    )(slots, before, *arrived)


def up16(value):
    return -(-value // 16) * 16


class Plan:
    def __init__(self, n_dp, rows, cap):
        self.n_dp, self.cap = n_dp, cap
        self.plane = n_dp // PLANES
        self.n_own = -(-n_dp // LANES) * LANES
        self.wide = -(-(cap + 1) // LANES) * LANES
        self.sent = self.wide + 3 * self.n_own + LANES
        self.early = rows // 2
        self.direct = up16(cap // 3)
        self.each = up16(cap // 3)
        self.near_cap = min(cap, up16(cap * 2 // 3))
        self.far = up16(rows * 11 // 64)


def shards(hidden, norm_gain, projection, centroids, owners, local_list, slot_table):
    n_dp = lax.axis_size("dp")
    me = lax.axis_index("tp").astype(I32)
    here = lax.axis_index("dp").astype(I32)
    rows = owners.shape[0]
    width = projection.shape[1]
    cap = slot_table.shape[1] // n_dp
    plan = Plan(n_dp, rows, cap)
    size = plan.plane
    gain = norm_gain.reshape(1, -1)
    groups = [list(range(q * size, (q + 1) * size)) for q in range(PLANES)]
    here = here.reshape(1)

    def across(blocks):
        pieces = len(blocks) // (PLANES - 1)
        return [
            lax.ppermute(
                block,
                "dp",
                [(p, ((p // size) ^ (1 + i // pieces)) * size + p % size) for p in range(n_dp)],
            )
            for i, block in enumerate(blocks)
        ]

    def exchange(blocks):
        return [blocks[0]] + [
            lax.ppermute(block, "dp", [(p, p - p % size + (p % size ^ k)) for p in range(n_dp)])
            for k, block in enumerate(blocks)
            if k > 0
        ]

    place, sent = route(plan, here, owners.reshape(1, rows), local_list.reshape(1, rows))
    heard = lax.all_to_all(
        sent.reshape(2 * n_dp, plan.sent), ("dp", "tp"), split_axis=0, concat_axis=0, tiled=True
    )
    def partials(chunk):
        half = rows // 2
        for_other = partial_keys((2 - 2 * me + chunk).reshape(1), hidden, gain, projection, half)
        other = lax.ppermute(for_other, "tp", [(0, 1), (1, 0)])
        own = partial_keys((2 * me + chunk).reshape(1), hidden, gain, projection, half)
        return own, other

    def direct(block):
        block = block.reshape(n_dp, -1, width)
        got = lax.all_to_all(block, "dp", split_axis=0, concat_axis=0, tiled=True)
        return got.reshape(-1, width)

    def fars(line):
        return [(line, e * FAR_STRIDE, plan.far) for e in range(PLANES - 1)]

    early_place = place[:, : plan.early]
    straight, early = pack([(3, 0, n_dp * plan.direct)], early_place, [], partials(0))
    straight = direct(straight)
    *far_first, late = pack(fars(0), place, [early], partials(1))
    far_first = across(far_first)
    nears = [(1, k * plan.near_cap, plan.near_cap) for k in range(size)]
    packed = pack(nears + fars(2), place, [early, late])
    near = exchange(packed[:size])
    far_second = across(packed[size:])

    level = jnp.max(heard[:, -1])
    heard = lax.dynamic_index_in_dim(heard.reshape(n_dp, 2, plan.sent), me, 1, keepdims=False)
    lists = heard[:, :cap].reshape(n_dp * cap)
    table = jnp.pad(slot_table.reshape(n_dp, cap), ((0, 0), (0, plan.wide - cap)))
    direct_slots, near_slots, first_slots, second_slots, third_slots, counts = wave_slots(
        plan, here, heard, table
    )
    centre = centres(slot_table.reshape(-1), lists, centroids)

    def flat(*parts):
        parts = [slots[:, :each].reshape(1, -1) for slots, each in parts]
        return jnp.concatenate(parts, axis=1) if len(parts) > 1 else parts[0]

    far_first, near, centre = lax.optimization_barrier((far_first, near, centre))
    passed = exchange(spread(plan, 0, here, counts, far_first))
    slots = flat((direct_slots, plan.direct), (near_slots, plan.near_cap))
    out = place_rows(slots, [straight, *near], centre)
    far_second, out = lax.optimization_barrier((far_second, out))
    blocks = spread(plan, 1, here, counts, far_second)
    blocks, passed = lax.optimization_barrier((blocks, passed))
    late_passed = exchange(blocks)
    slots = flat((first_slots, plan.each), (second_slots[: PLANES - 1], plan.each))
    out = place_rows(slots, [*passed, blocks[0]], out)
    slots = flat((second_slots[PLANES - 1 :], plan.each))

    def finish(args):
        return place_rows(args["slots"], args["rows"], args["out"])

    def finish_more(size):
        def branch(args):
            third = args["place"][4:5]
            third = jnp.where(third < 0, -1, third // cap * size + third % cap)
            third = jnp.broadcast_to(third, args["place"].shape)
            (more,) = pack([(0, 0, n_dp * size)], third, args["keys"])
            return place_rows(flat((args["third_slots"], size)), [direct(more)], finish(args))

        return branch

    few = up16(cap // 3)
    return lax.switch(
        (level > 0).astype(I32) + (level > few).astype(I32),
        [finish, finish_more(few), finish_more(cap)],
        dict(
            slots=slots, rows=late_passed[1:], out=out, place=place, keys=[early, late],
            third_slots=third_slots,
        ),
    )


def solution(mesh):
    placed = (
        P("dp", "tp"),
        P("tp"),
        P("tp", None),
        P("dp", None),
        P(("dp", "tp"), None),
        P(("dp", "tp")),
        P(("dp", "tp"), None),
    )
    return jax.shard_map(
        shards, mesh=mesh, in_specs=placed, out_specs=P(("dp", "tp"), None), check_vma=False
    )
```

profile of v0, /device:TPU:21, one launch (start us, length us, event | category | flops | bytes accessed | tf_op | source)
XLA Modules:
  0.0 194.4 jit_solution(6028115571206168812)
XLA Ops:
  1.3 9.2 %partial_keys.5 = bf16[512,1280]{1,0:T(8,128)(2,1)} custom-call(s32[1]{0:T(128)} %bitcast.10.which, bf16[2048,4096]{1,0:T(8,128)(2,1)} %hidden.7, bf16[1,4096]{1,0:T(2,128)(2,1)} %reshape.89.gain, bf16[4096,1024]{1,0:T(8,128)(2,1)} %projection.7), custom_call_target="tpu_custom_call" | custom-call | flops 4294967296 | bytes 13631488 | tf_op jit(solution)/shard_map/partial_keys/pallas_call | solution.py:78
  13.2 5.7 %all-to-all-start.2 = ((s32[32,1,768]{2,1,0:T(1,128)}), s32[32,1,768]{2,1,0:T(1,128)S(1)}, u32[]{:S(2)}, u32[]{:S(2)}) async-start(s32[32,1,768]{2,1,0:T(1,128)} %all_to_all.21), calls=%async_computation.2 | async-start | bytes 196608 | tf_op jit(solution)/shard_map/all_to_all | solution.py:592
  18.9 9.2 %partial_keys.4.refs_0_ = bf16[512,1280]{1,0:T(8,128)(2,1)} custom-call(s32[1]{0:T(128)} %bitcast.9.which, bf16[2048,4096]{1,0:T(8,128)(2,1)} %hidden.7, bf16[1,4096]{1,0:T(2,128)(2,1)} %reshape.89.gain, bf16[4096,1024]{1,0:T(8,128)(2,1)} %projection.7), custom_call_target="tpu_custom_call" | custom-call | flops 4294967296 | bytes 13631488 | tf_op jit(solution)/shard_map/partial_keys/pallas_call | solution.py:78
  29.7 4.9 %pack_keys.7 = (bf16[1024,1024]{1,0:T(8,128)(2,1)}, bf16[512,1024]{1,0:T(8,128)(2,1)S(1)}) custom-call(s32[8,512]{1,0:T(8,128)} %slice.44.place, bf16[512,1280]{1,0:T(8,128)(2,1)} %partial_keys.4.refs_0_, bf16[512,1280]{1,0:T(8,128)(2,1)} %copy-done.5), custom_call_target="tpu_custom_call" | custom-call | flops 1 | bytes 1 | tf_op jit(solution)/shard_map/pack_keys/pallas_call | solution.py:359
  34.6 6.4 %all-to-all-start.3 = ((bf16[16,64,1024]{2,1,0:T(8,128)(2,1)}), bf16[16,64,1024]{2,1,0:T(8,128)(2,1)}, u32[]{:S(2)}, u32[]{:S(2)}) async-start(bf16[16,64,1024]{2,1,0:T(8,128)(2,1)} %bitcast.31), calls=%async_computation.3 | async-start | bytes 4194304 | tf_op jit(solution)/shard_map/all_to_all | solution.py:604
  41.1 9.2 %partial_keys.7 = bf16[512,1280]{1,0:T(8,128)(2,1)} custom-call(s32[1]{0:T(128)} %bitcast.12.which, bf16[2048,4096]{1,0:T(8,128)(2,1)} %hidden.7, bf16[1,4096]{1,0:T(2,128)(2,1)} %reshape.89.gain, bf16[4096,1024]{1,0:T(8,128)(2,1)} %projection.7), custom_call_target="tpu_custom_call" | custom-call | flops 4294967296 | bytes 13631488 | tf_op jit(solution)/shard_map/partial_keys/pallas_call | solution.py:78
  51.2 9.2 %partial_keys.6.refs_1_ = bf16[512,1280]{1,0:T(8,128)(2,1)} custom-call(s32[1]{0:T(128)} %bitcast.11.which, bf16[2048,4096]{1,0:T(8,128)(2,1)} %hidden.7, bf16[1,4096]{1,0:T(2,128)(2,1)} %reshape.89.gain, bf16[4096,1024]{1,0:T(8,128)(2,1)} %projection.7), custom_call_target="tpu_custom_call" | custom-call | flops 4294967296 | bytes 13631488 | tf_op jit(solution)/shard_map/partial_keys/pallas_call | solution.py:78
  61.5 4.4 %pack_keys.8 = (bf16[176,1024]{1,0:T(8,128)(2,1)}, bf16[176,1024]{1,0:T(8,128)(2,1)}, bf16[176,1024]{1,0:T(8,128)(2,1)}, bf16[512,1024]{1,0:T(8,128)(2,1)S(1)}) custom-call(s32[8,1024]{1,0:T(8,128)S(1)} %get-tuple-element.130.place, bf16[512,1024]{1,0:T(8,128)(2,1)S(1)} %get-tuple-element.131.refs_0_, bf16[512,1280]{1,0:T(8,128)(2,1)} %partial_keys.6.refs_1_, ...), custom_call_target="tpu_custom_call" | custom-call | flops 1 | bytes 1 | tf_op jit(solution)/shard_map/pack_keys/pallas_call | solution.py:359
  65.8 3.3 %pack_keys.9 = (bf16[128,1024]{1,0:T(8,128)(2,1)}, bf16[128,1024]{1,0:T(8,128)(2,1)}, bf16[128,1024]{1,0:T(8,128)(2,1)}, bf16[128,1024]{1,0:T(8,128)(2,1)}, bf16...) custom-call(s32[8,1024]{1,0:T(8,128)S(1)} %get-tuple-element.130.place, ...), custom_call_target="tpu_custom_call" | custom-call | flops 1 | bytes 1 | tf_op jit(solution)/shard_map/pack_keys/pallas_call | solution.py:359
  76.0 11.0 %collective-permute-done.8.refs_2_ = bf16[128,1024]{1,0:T(8,128)(2,1)} collective-permute-done((bf16[128,1024]{1,0:T(8,128)(2,1)}, bf16[128,1024]{1,0:T(8,128)(2,1)}, u32[]{:S(2)}, u32[]{:S(2)}) %collective-permute-start.8) | collective-permute-done | bytes 262176 | tf_op jit(solution)/shard_map/ppermute | solution.py:586
  87.0 1.9 collective-permute-start.10
  89.8 1.5 wave_slots.1
  92.6 18.6 %centroid_rows.1.before = bf16[3072,1024]{1,0:T(8,128)(2,1)} custom-call(s32[3072]{0:T(1024)} %bitcast.33, s32[3072]{0:T(1024)} %fusion.2.lists, bf16[4096,1024]{1,0:T(8,128)(2,1)} %centroids.1), custom_call_target="tpu_custom_call" | custom-call | flops 1 | bytes 1 | tf_op jit(solution)/shard_map/centroid_rows/pallas_call | solution.py:475
  111.3 7.9 %collective-permute-done.7.refs_2_ = bf16[176,1024]{1,0:T(8,128)(2,1)S(1)} collective-permute-done((bf16[176,1024]{1,0:T(8,128)(2,1)}, bf16[176,1024]{1,0:T(8,128)(2,1)S(1)}, u32[]{:S(2)}, u32[]{:S(2)}) %collective-permute-start.7) | collective-permute-done | bytes 360480 | tf_op jit(solution)/shard_map/ppermute | solution.py:576
  119.9 4.1 %spread_rows.3 = (bf16[192,1024]{1,0:T(8,128)(2,1)}, bf16[192,1024]{1,0:T(8,128)(2,1)}, bf16[192,1024]{1,0:T(8,128)(2,1)}, bf16[192,1024]{1,0:T(8,128)(2,1)}) custom-call(s32[1]{0:T(128)} %bitcast.6.me, s32[8,128]{1,0:T(8,128)} %copy-done, bf16[176,1024]{1,0:T(8,128)(2,1)} %copy-done.9, bf16[176,1024]{1,0:T(8,128)(2,1)} %copy-done.10, ...), custom_call_target="tpu_custom_call" | custom-call | flops 1 | bytes 1 | tf_op jit(solution)/shard_map/spread_rows/pallas_call | solution.py:401
  124.8 1.8 collective-permute-start.13
  128.3 15.1 %residual_rows.12.before = bf16[3072,1024]{1,0:T(8,128)(2,1)} custom-call(s32[1,1536]{1,0:T(1,128)} %pad_add_fusion.slots, bf16[3072,1024]{1,0:T(8,128)(2,1)} %centroid_rows.1.before, bf16[1024,1024]{1,0:T(8,128)(2,1)} %bitcast.16.refs_0_, bf16[128,1024]{1,0:T(8,128)(2,1)} %get-tuple-element.147.refs_1_, bf16[128,1024]{1,0:T(8,128)(2,1)} %collective-permute-done.8.refs_2_, ...), custom_call_target="tpu_custom_call" | custom-call | flops 1 | bytes 1 | tf_op jit(solution)/shard_map/residual_rows/pallas_call | solution.py:522
  143.4 5.2 %collective-permute-done.3.refs_1_ = bf16[176,1024]{1,0:T(8,128)(2,1)} collective-permute-done((bf16[176,1024]{1,0:T(8,128)(2,1)}, bf16[176,1024]{1,0:T(8,128)(2,1)}, u32[]{:S(2)}, u32[]{:S(2)}) %collective-permute-start.3) | collective-permute-done | bytes 360480 | tf_op jit(solution)/shard_map/ppermute | solution.py:576
  148.6 9.9 %collective-permute-done.4.refs_2_ = bf16[176,1024]{1,0:T(8,128)(2,1)} collective-permute-done((bf16[176,1024]{1,0:T(8,128)(2,1)}, bf16[176,1024]{1,0:T(8,128)(2,1)}, u32[]{:S(2)}, u32[]{:S(2)}) %collective-permute-start.4) | collective-permute-done | bytes 360480 | tf_op jit(solution)/shard_map/ppermute | solution.py:576
  158.5 4.3 %spread_rows.2 = (bf16[192,1024]{1,0:T(8,128)(2,1)}, bf16[192,1024]{1,0:T(8,128)(2,1)}, bf16[192,1024]{1,0:T(8,128)(2,1)}, bf16[192,1024]{1,0:T(8,128)(2,1)}) custom-call(s32[1]{0:T(128)} %bitcast.6.me, s32[8,128]{1,0:T(8,128)} %copy-done, bf16[176,1024]{1,0:T(8,128)(2,1)} %collective-permute-done.2.refs_0_, ...), custom_call_target="tpu_custom_call" | custom-call | flops 1 | bytes 1 | tf_op jit(solution)/shard_map/spread_rows/pallas_call | solution.py:401
  163.9 2.5 %collective-permute-start.16 = (bf16[192,1024]{1,0:T(8,128)(2,1)}, bf16[192,1024]{1,0:T(8,128)(2,1)S(1)}, u32[]{:S(2)}, u32[]{:S(2)}) collective-permute-start(bf16[192,1024]{1,0:T(8,128)(2,1)} %get-tuple-element.174), channel_id=1, source_target_pairs={{0,3},{1,2},{2,1},{3,0},{4,7},{5,6},{6,5},{7,4},{8,11},{9,10},{10,... | collective-permute-start | bytes 1179656 | tf_op jit(solution)/shard_map/ppermute | solution.py:586
  171.8 12.3 %residual_rows.13 = bf16[3072,1024]{1,0:T(8,128)(2,1)} custom-call(s32[1,960]{1,0:T(1,128)} %pad_add_fusion.1.slots, bf16[3072,1024]{1,0:T(8,128)(2,1)} %residual_rows.12.before, bf16[192,1024]{1,0:T(8,128)(2,1)} %get-tuple-element.167.refs_0_, bf16[192,1024]{1,0:T(8,128)(2,1)} %copy-done.6, bf16[192,1024]{1,0:T(8,128)(2,1)} %copy-done.7, ...), custom_call_target="tpu_custom_call" | custom-call | flops 1 | bytes 1 | tf_op jit(solution)/shard_map/residual_rows/pallas_call | solution.py:522
  184.1 10.2 %conditional.1 = (bf16[3072,1024]{1,0:T(8,128)(2,1)}) conditional(s32[]{:T(128)} %clamp.3, (s32[1,576]{1,0:T(1,128)S(1)}, bf16[3072,1024]{1,0:T(8,128)(2,1)}, bf16[192,1024]{1,0:T(8,128)(2,1)S(1)}, bf16[192,1024]{1,0:T(8,128)(2,1)S(1)}, bf16[192,1024]{1,0:T(8,128)(2,1)S(1)}) %tuple.20, (s32[16,256]{1,0:T(8,128)S(1)}, ...), branch_computations={%region_1.2_spmd, %region_2.3_spmd, %region_3.4_spmd} | conditional | flops 16387 | bytes 18944044 | solution.py:659
  184.1 10.2 %residual_rows.7 = bf16[3072,1024]{1,0:T(8,128)(2,1)} custom-call(s32[1,576]{1,0:T(1,128)S(1)} %get-tuple-element.54.slots, bf16[3072,1024]{1,0:T(8,128)(2,1)} %get-tuple-element.56.before, bf16[192,1024]{1,0:T(8,128)(2,1)S(1)} %get-tuple-element.57.refs_0_, bf16[192,1024]{1,0:T(8,128)(2,1)S(1)} %get-tuple-element.58.refs_1_, ...), custom_call_target="tpu_custom_call" | custom-call | flops 1 | bytes 1 | tf_op jit(solution)/shard_map/cond/branch_0_fun/residual_rows/pallas_call | solution.py:522
  (81 shorter events, 25.2 us)
Async XLA Ops:
  1.3 9.9 %copy-start.1 = (s32[1024,1]{0,1:T(1,128)S(1)}, s32[1024,1]{0,1:T(1,128)}, u32[]{:S(2)}) copy-start(s32[1024,1]{0,1:T(1,128)} %param.14) | copy-start | bytes 12292
  1.3 9.9 %copy-start.2 = (s32[1024]{0:T(1024)S(1)}, s32[1024]{0:T(1024)}, u32[]{:S(2)}) copy-start(s32[1024]{0:T(1024)} %param.15) | copy-start | bytes 12292
  10.5 18.1 %collective-permute-start = (bf16[512,1280]{1,0:T(8,128)(2,1)}, bf16[512,1280]{1,0:T(8,128)(2,1)S(1)}, u32[]{:S(2)}, u32[]{:S(2)}) collective-permute-start(bf16[512,1280]{1,0:T(8,128)(2,1)} %partial_keys.5), channel_id=1, source_target_pairs={{0,16},{16,0},{1,17},{17,1},{2,18},{18,2},{3,19},{19,3},{4,20},{20... | collective-permute-start | bytes 3932168 | tf_op jit(solution)/shard_map/ppermute | solution.py:598
  13.2 21.4 %all-to-all-start.2 = ((s32[32,1,768]{2,1,0:T(1,128)}), s32[32,1,768]{2,1,0:T(1,128)S(1)}, u32[]{:S(2)}, u32[]{:S(2)}) async-start(s32[32,1,768]{2,1,0:T(1,128)} %all_to_all.21), calls=%async_computation.2 | async-start | bytes 196608 | tf_op jit(solution)/shard_map/all_to_all | solution.py:592
  34.6 93.7 %all-to-all-start.3 = ((bf16[16,64,1024]{2,1,0:T(8,128)(2,1)}), bf16[16,64,1024]{2,1,0:T(8,128)(2,1)}, u32[]{:S(2)}, u32[]{:S(2)}) async-start(bf16[16,64,1024]{2,1,0:T(8,128)(2,1)} %bitcast.31), calls=%async_computation.3 | async-start | bytes 4194304 | tf_op jit(solution)/shard_map/all_to_all | solution.py:604
  50.3 10.1 %collective-permute-start.1 = (bf16[512,1280]{1,0:T(8,128)(2,1)}, bf16[512,1280]{1,0:T(8,128)(2,1)S(1)}, u32[]{:S(2)}, u32[]{:S(2)}) collective-permute-start(bf16[512,1280]{1,0:T(8,128)(2,1)} %partial_keys.7), channel_id=1, source_target_pairs={{0,16},{16,0},{1,17},{17,1},{2,18},{18,2},{3,19},{19,3},{4,20},{20... | collective-permute-start | bytes 3932168 | tf_op jit(solution)/shard_map/ppermute | solution.py:598
  51.2 22.6 %copy-start.12 = (s32[1,3072]{1,0:T(1,128)S(1)}, s32[1,3072]{1,0:T(1,128)}, u32[]{:S(2)}) copy-start(s32[1,3072]{1,0:T(1,128)} %param.16) | copy-start | bytes 36868
  69.1 17.9 %collective-permute-start.8 = (bf16[128,1024]{1,0:T(8,128)(2,1)}, bf16[128,1024]{1,0:T(8,128)(2,1)}, u32[]{:S(2)}, u32[]{:S(2)}) collective-permute-start(bf16[128,1024]{1,0:T(8,128)(2,1)} %get-tuple-element.142), channel_id=1, source_target_pairs={{0,1},{1,0},{2,3},{3,2},{4,5},{5,4},{6,7},{7,6},{8,9},{9,8},{10,11... | collective-permute-start | bytes 786440 | tf_op jit(solution)/shard_map/ppermute | solution.py:586
  70.3 18.6 %collective-permute-start.9 = (bf16[128,1024]{1,0:T(8,128)(2,1)}, bf16[128,1024]{1,0:T(8,128)(2,1)}, u32[]{:S(2)}, u32[]{:S(2)}) collective-permute-start(bf16[128,1024]{1,0:T(8,128)(2,1)} %get-tuple-element.143), channel_id=1, source_target_pairs={{0,2},{1,3},{2,0},{3,1},{4,6},{5,7},{6,4},{7,5},{8,10},{9,11},{10,... | collective-permute-start | bytes 786440 | tf_op jit(solution)/shard_map/ppermute | solution.py:586
  70.6 40.7 %collective-permute-start.5 = (bf16[176,1024]{1,0:T(8,128)(2,1)}, bf16[176,1024]{1,0:T(8,128)(2,1)S(1)}, u32[]{:S(2)}, u32[]{:S(2)}) collective-permute-start(bf16[176,1024]{1,0:T(8,128)(2,1)} %get-tuple-element.138), channel_id=1, source_target_pairs={{0,4},{1,5},{2,6},{3,7},{4,0},{5,1},{6,2},{7,3},{8,12},{9,13},{10,... | collective-permute-start | bytes 1081352 | tf_op jit(solution)/shard_map/ppermute | solution.py:576
  71.8 39.5 %collective-permute-start.6 = (bf16[176,1024]{1,0:T(8,128)(2,1)}, bf16[176,1024]{1,0:T(8,128)(2,1)S(1)}, u32[]{:S(2)}, u32[]{:S(2)}) collective-permute-start(bf16[176,1024]{1,0:T(8,128)(2,1)} %get-tuple-element.139), channel_id=1, source_target_pairs={{0,8},{1,9},{2,10},{3,11},{4,12},{5,13},{6,14},{7,15},{8,0},{9,1},... | collective-permute-start | bytes 1081352 | tf_op jit(solution)/shard_map/ppermute | solution.py:576
  72.0 47.1 %collective-permute-start.7 = (bf16[176,1024]{1,0:T(8,128)(2,1)}, bf16[176,1024]{1,0:T(8,128)(2,1)S(1)}, u32[]{:S(2)}, u32[]{:S(2)}) collective-permute-start(bf16[176,1024]{1,0:T(8,128)(2,1)} %get-tuple-element.140), channel_id=1, source_target_pairs={{0,12},{1,13},{2,14},{3,15},{4,8},{5,9},{6,10},{7,11},{8,4},{9,5},... | collective-permute-start | bytes 1081352 | tf_op jit(solution)/shard_map/ppermute | solution.py:576
  87.0 24.2 %collective-permute-start.10 = (bf16[128,1024]{1,0:T(8,128)(2,1)}, bf16[128,1024]{1,0:T(8,128)(2,1)}, u32[]{:S(2)}, u32[]{:S(2)}) collective-permute-start(bf16[128,1024]{1,0:T(8,128)(2,1)} %get-tuple-element.144), channel_id=1, source_target_pairs={{0,3},{1,2},{2,1},{3,0},{4,7},{5,6},{6,5},{7,4},{8,11},{9,10},{10,... | collective-permute-start | bytes 786440 | tf_op jit(solution)/shard_map/ppermute | solution.py:586
  88.9 37.8 %collective-permute-start.2 = (bf16[176,1024]{1,0:T(8,128)(2,1)}, bf16[176,1024]{1,0:T(8,128)(2,1)}, u32[]{:S(2)}, u32[]{:S(2)}) collective-permute-start(bf16[176,1024]{1,0:T(8,128)(2,1)} %get-tuple-element.133), channel_id=1, source_target_pairs={{0,4},{1,5},{2,6},{3,7},{4,0},{5,1},{6,2},{7,3},{8,12},{9,13},{10,... | collective-permute-start | bytes 1081352 | tf_op jit(solution)/shard_map/ppermute | solution.py:576
  111.3 7.9 %copy-start.9 = (bf16[176,1024]{1,0:T(8,128)(2,1)}, bf16[176,1024]{1,0:T(8,128)(2,1)S(1)}, u32[]{:S(2)}) copy-start(bf16[176,1024]{1,0:T(8,128)(2,1)S(1)} %collective-permute-done.5.refs_0_) | copy-start | bytes 1081348
  111.3 7.9 %copy-start.10 = (bf16[176,1024]{1,0:T(8,128)(2,1)}, bf16[176,1024]{1,0:T(8,128)(2,1)S(1)}, u32[]{:S(2)}) copy-start(bf16[176,1024]{1,0:T(8,128)(2,1)S(1)} %collective-permute-done.6.refs_1_) | copy-start | bytes 1081348
  124.0 38.8 %collective-permute-start.11 = (bf16[192,1024]{1,0:T(8,128)(2,1)}, bf16[192,1024]{1,0:T(8,128)(2,1)S(1)}, u32[]{:S(2)}, u32[]{:S(2)}) collective-permute-start(bf16[192,1024]{1,0:T(8,128)(2,1)} %get-tuple-element.164), channel_id=1, source_target_pairs={{0,1},{1,0},{2,3},{3,2},{4,5},{5,4},{6,7},{7,6},{8,9},{9,8},{10,11... | collective-permute-start | bytes 1179656 | tf_op jit(solution)/shard_map/ppermute | solution.py:586
  124.8 38.0 %collective-permute-start.12 = (bf16[192,1024]{1,0:T(8,128)(2,1)}, bf16[192,1024]{1,0:T(8,128)(2,1)S(1)}, u32[]{:S(2)}, u32[]{:S(2)}) collective-permute-start(bf16[192,1024]{1,0:T(8,128)(2,1)} %get-tuple-element.165), channel_id=1, source_target_pairs={{0,2},{1,3},{2,0},{3,1},{4,6},{5,7},{6,4},{7,5},{8,10},{9,11},{10,... | collective-permute-start | bytes 1179656 | tf_op jit(solution)/shard_map/ppermute | solution.py:586
  124.8 38.0 %collective-permute-start.13 = (bf16[192,1024]{1,0:T(8,128)(2,1)}, bf16[192,1024]{1,0:T(8,128)(2,1)S(1)}, u32[]{:S(2)}, u32[]{:S(2)}) collective-permute-start(bf16[192,1024]{1,0:T(8,128)(2,1)} %get-tuple-element.166), channel_id=1, source_target_pairs={{0,3},{1,2},{2,1},{3,0},{4,7},{5,6},{6,5},{7,4},{8,11},{9,10},{10,... | collective-permute-start | bytes 1179656 | tf_op jit(solution)/shard_map/ppermute | solution.py:586
  126.6 22.0 %collective-permute-start.3 = (bf16[176,1024]{1,0:T(8,128)(2,1)}, bf16[176,1024]{1,0:T(8,128)(2,1)}, u32[]{:S(2)}, u32[]{:S(2)}) collective-permute-start(bf16[176,1024]{1,0:T(8,128)(2,1)} %get-tuple-element.134), channel_id=1, source_target_pairs={{0,8},{1,9},{2,10},{3,11},{4,12},{5,13},{6,14},{7,15},{8,0},{9,1},... | collective-permute-start | bytes 1081352 | tf_op jit(solution)/shard_map/ppermute | solution.py:576
  126.6 31.9 %collective-permute-start.4 = (bf16[176,1024]{1,0:T(8,128)(2,1)}, bf16[176,1024]{1,0:T(8,128)(2,1)}, u32[]{:S(2)}, u32[]{:S(2)}) collective-permute-start(bf16[176,1024]{1,0:T(8,128)(2,1)} %get-tuple-element.135), channel_id=1, source_target_pairs={{0,12},{1,13},{2,14},{3,15},{4,8},{5,9},{6,10},{7,11},{8,4},{9,5},... | collective-permute-start | bytes 1081352 | tf_op jit(solution)/shard_map/ppermute | solution.py:576
  163.7 20.4 %collective-permute-start.14 = (bf16[192,1024]{1,0:T(8,128)(2,1)}, bf16[192,1024]{1,0:T(8,128)(2,1)S(1)}, u32[]{:S(2)}, u32[]{:S(2)}) collective-permute-start(bf16[192,1024]{1,0:T(8,128)(2,1)} %get-tuple-element.172), channel_id=1, source_target_pairs={{0,1},{1,0},{2,3},{3,2},{4,5},{5,4},{6,7},{7,6},{8,9},{9,8},{10,11... | collective-permute-start | bytes 1179656 | tf_op jit(solution)/shard_map/ppermute | solution.py:586
  163.8 20.2 %collective-permute-start.15 = (bf16[192,1024]{1,0:T(8,128)(2,1)}, bf16[192,1024]{1,0:T(8,128)(2,1)S(1)}, u32[]{:S(2)}, u32[]{:S(2)}) collective-permute-start(bf16[192,1024]{1,0:T(8,128)(2,1)} %get-tuple-element.173), channel_id=1, source_target_pairs={{0,2},{1,3},{2,0},{3,1},{4,6},{5,7},{6,4},{7,5},{8,10},{9,11},{10,... | collective-permute-start | bytes 1179656 | tf_op jit(solution)/shard_map/ppermute | solution.py:586
  163.9 20.2 %collective-permute-start.16 = (bf16[192,1024]{1,0:T(8,128)(2,1)}, bf16[192,1024]{1,0:T(8,128)(2,1)S(1)}, u32[]{:S(2)}, u32[]{:S(2)}) collective-permute-start(bf16[192,1024]{1,0:T(8,128)(2,1)} %get-tuple-element.174), channel_id=1, source_target_pairs={{0,3},{1,2},{2,1},{3,0},{4,7},{5,6},{6,5},{7,4},{8,11},{9,10},{10,... | collective-permute-start | bytes 1179656 | tf_op jit(solution)/shard_map/ppermute | solution.py:586
  (7 other events, 6.1 us)
where the time goes:
time: 198 us; the launch traced here: 194 us
  Pallas kernels  117 us (59%)
  waiting for transfers between devices  34 us (17%)
  starting transfers between devices  25.8 us (13%)
  local copies, waits for them, and re-layouts  12.3 us (6%)
  other arithmetic  4.05 us (2%)
    pallas_call x3, Pallas kernels, place_rows(): pl.pallas_call(functools.partial(place_kernel, sizes), grid=(count // til...  37.5 us
    pallas_call x4, Pallas kernels, partial_keys(): pl.pallas_call(partial_kernel, grid_spec=pltpu.PrefetchScalarGridSpec(num...  36.8 us
    ppermute x6, waiting for transfers between devices, across(): lax.ppermute(block, 'dp', [(p, (p // size ^ 1 + i // pieces) * size + p %...  23 us
    pallas_call x1, Pallas kernels, centres(): pl.pallas_call(functools.partial(centre_kernel, n_in), grid_spec=pltpu.Pr...  18.6 us
    pallas_call x3, Pallas kernels, pack(): pl.pallas_call(functools.partial(pack_kernel, moves, len(keys), bool(fres...  12.6 us
    ppermute x9, waiting for transfers between devices, exchange(): lax.ppermute(block, 'dp', [(p, p - p % size + (p % size ^ k)) for p in ra...  11 us
    ppermute x9, starting transfers between devices, exchange(): lax.ppermute(block, 'dp', [(p, p - p % size + (p % size ^ k)) for p in ra...  8.48 us
    pallas_call x2, Pallas kernels, spread(): pl.pallas_call(functools.partial(spread_kernel, plan, wave), grid_spec=pl...  8.35 us
  transfers between devices with their start and end apart: 19, of which 4 were waited for; matrix products, arithmetic and copies ran while one was open for 5% of the time, Pallas kernels for 50%

commit v1 on v0

--- a/solution.py
+++ b/solution.py
@@ -554,7 +554,7 @@
         self.direct = up16(cap // 3)
         self.each = up16(cap // 3)
         self.near_cap = min(cap, up16(cap * 2 // 3))
-        self.far = up16(rows * 11 // 64)
+        self.far = up16(rows * 5 // 32)
 
 
 def shards(hidden, norm_gain, projection, centroids, owners, local_list, slot_table):

time: 198 us -> 192 us (0.970)
  waiting for transfers between devices: 34 us -> 29.8 us
    ppermute x6, waiting for transfers between devices: 23 us -> 18.1 us  [across(): lax.ppermute(block, 'dp', [(p, (p // size ^ 1 + i // pieces) * size + p %...]
  transfers between devices with their start and end apart: 19 -> 19, of which waited for: 4 -> 4; matrix products, arithmetic and copies ran while one was open for 5% -> 4% of each run, Pallas kernels for 50% -> 51%
where the time goes in v1:
time: 192 us; the launch traced here: 189 us
  Pallas kernels  116 us (60%)
  waiting for transfers between devices  29.8 us (16%)
  starting transfers between devices  25.9 us (13%)
  local copies, waits for them, and re-layouts  10.8 us (6%)
  other arithmetic  4.1 us (2%)
    pallas_call x3, Pallas kernels, place_rows(): pl.pallas_call(functools.partial(place_kernel, sizes), grid=(count // til...  37.5 us
    pallas_call x4, Pallas kernels, partial_keys(): pl.pallas_call(partial_kernel, grid_spec=pltpu.PrefetchScalarGridSpec(num...  36.8 us
    pallas_call x1, Pallas kernels, centres(): pl.pallas_call(functools.partial(centre_kernel, n_in), grid_spec=pltpu.Pr...  18.6 us
    ppermute x6, waiting for transfers between devices, across(): lax.ppermute(block, 'dp', [(p, (p // size ^ 1 + i // pieces) * size + p %...  18.1 us
    pallas_call x3, Pallas kernels, pack(): pl.pallas_call(functools.partial(pack_kernel, moves, len(keys), bool(fres...  12.3 us
    ppermute x9, waiting for transfers between devices, exchange(): lax.ppermute(block, 'dp', [(p, p - p % size + (p % size ^ k)) for p in ra...  11.7 us
    ppermute x9, starting transfers between devices, exchange(): lax.ppermute(block, 'dp', [(p, p - p % size + (p % size ^ k)) for p in ra...  8.58 us
    pallas_call x2, Pallas kernels, spread(): pl.pallas_call(functools.partial(spread_kernel, plan, wave), grid_spec=pl...  8.27 us
  transfers between devices with their start and end apart: 19, of which 4 were waited for; matrix products, arithmetic and copies ran while one was open for 4% of the time, Pallas kernels for 51%

profile of v1, /device:TPU:21, one launch (start us, length us, event | category | flops | bytes accessed | tf_op | source)
XLA Modules:
  0.0 188.6 jit_solution(9088156478975271633)
XLA Ops:
  1.3 9.2 %partial_keys.5 = bf16[512,1280]{1,0:T(8,128)(2,1)} custom-call(s32[1]{0:T(128)} %bitcast.10.which, bf16[2048,4096]{1,0:T(8,128)(2,1)} %hidden.7, bf16[1,4096]{1,0:T(2,128)(2,1)} %reshape.89.gain, bf16[4096,1024]{1,0:T(8,128)(2,1)} %projection.7), custom_call_target="tpu_custom_call" | custom-call | flops 4294967296 | bytes 13631488 | tf_op jit(solution)/shard_map/partial_keys/pallas_call | solution.py:78
  13.2 5.7 %all-to-all-start.2 = ((s32[32,1,768]{2,1,0:T(1,128)}), s32[32,1,768]{2,1,0:T(1,128)S(1)}, u32[]{:S(2)}, u32[]{:S(2)}) async-start(s32[32,1,768]{2,1,0:T(1,128)} %all_to_all.21), calls=%async_computation.2 | async-start | bytes 196608 | tf_op jit(solution)/shard_map/all_to_all | solution.py:592
  18.9 9.2 %partial_keys.4.refs_0_ = bf16[512,1280]{1,0:T(8,128)(2,1)} custom-call(s32[1]{0:T(128)} %bitcast.9.which, bf16[2048,4096]{1,0:T(8,128)(2,1)} %hidden.7, bf16[1,4096]{1,0:T(2,128)(2,1)} %reshape.89.gain, bf16[4096,1024]{1,0:T(8,128)(2,1)} %projection.7), custom_call_target="tpu_custom_call" | custom-call | flops 4294967296 | bytes 13631488 | tf_op jit(solution)/shard_map/partial_keys/pallas_call | solution.py:78
  29.7 4.9 %pack_keys.7 = (bf16[1024,1024]{1,0:T(8,128)(2,1)}, bf16[512,1024]{1,0:T(8,128)(2,1)S(1)}) custom-call(s32[8,512]{1,0:T(8,128)} %slice.44.place, bf16[512,1280]{1,0:T(8,128)(2,1)} %partial_keys.4.refs_0_, bf16[512,1280]{1,0:T(8,128)(2,1)} %copy-done.5), custom_call_target="tpu_custom_call" | custom-call | flops 1 | bytes 1 | tf_op jit(solution)/shard_map/pack_keys/pallas_call | solution.py:359
  34.6 6.4 %all-to-all-start.3 = ((bf16[16,64,1024]{2,1,0:T(8,128)(2,1)}), bf16[16,64,1024]{2,1,0:T(8,128)(2,1)}, u32[]{:S(2)}, u32[]{:S(2)}) async-start(bf16[16,64,1024]{2,1,0:T(8,128)(2,1)} %bitcast.31), calls=%async_computation.3 | async-start | bytes 4194304 | tf_op jit(solution)/shard_map/all_to_all | solution.py:604
  41.1 9.2 %partial_keys.7 = bf16[512,1280]{1,0:T(8,128)(2,1)} custom-call(s32[1]{0:T(128)} %bitcast.12.which, bf16[2048,4096]{1,0:T(8,128)(2,1)} %hidden.7, bf16[1,4096]{1,0:T(2,128)(2,1)} %reshape.89.gain, bf16[4096,1024]{1,0:T(8,128)(2,1)} %projection.7), custom_call_target="tpu_custom_call" | custom-call | flops 4294967296 | bytes 13631488 | tf_op jit(solution)/shard_map/partial_keys/pallas_call | solution.py:78
  51.2 9.2 %partial_keys.6.refs_1_ = bf16[512,1280]{1,0:T(8,128)(2,1)} custom-call(s32[1]{0:T(128)} %bitcast.11.which, bf16[2048,4096]{1,0:T(8,128)(2,1)} %hidden.7, bf16[1,4096]{1,0:T(2,128)(2,1)} %reshape.89.gain, bf16[4096,1024]{1,0:T(8,128)(2,1)} %projection.7), custom_call_target="tpu_custom_call" | custom-call | flops 4294967296 | bytes 13631488 | tf_op jit(solution)/shard_map/partial_keys/pallas_call | solution.py:78
  61.5 4.2 %pack_keys.8 = (bf16[160,1024]{1,0:T(8,128)(2,1)}, bf16[160,1024]{1,0:T(8,128)(2,1)}, bf16[160,1024]{1,0:T(8,128)(2,1)}, bf16[512,1024]{1,0:T(8,128)(2,1)S(1)}) custom-call(s32[8,1024]{1,0:T(8,128)S(1)} %get-tuple-element.130.place, bf16[512,1024]{1,0:T(8,128)(2,1)S(1)} %get-tuple-element.131.refs_0_, bf16[512,1280]{1,0:T(8,128)(2,1)} %partial_keys.6.refs_1_, ...), custom_call_target="tpu_custom_call" | custom-call | flops 1 | bytes 1 | tf_op jit(solution)/shard_map/pack_keys/pallas_call | solution.py:359
  65.7 3.2 %pack_keys.9 = (bf16[128,1024]{1,0:T(8,128)(2,1)}, bf16[128,1024]{1,0:T(8,128)(2,1)}, bf16[128,1024]{1,0:T(8,128)(2,1)}, bf16[128,1024]{1,0:T(8,128)(2,1)}, bf16...) custom-call(s32[8,1024]{1,0:T(8,128)S(1)} %get-tuple-element.130.place, ...), custom_call_target="tpu_custom_call" | custom-call | flops 1 | bytes 1 | tf_op jit(solution)/shard_map/pack_keys/pallas_call | solution.py:359
  75.3 11.7 %collective-permute-done.8.refs_2_ = bf16[128,1024]{1,0:T(8,128)(2,1)} collective-permute-done((bf16[128,1024]{1,0:T(8,128)(2,1)}, bf16[128,1024]{1,0:T(8,128)(2,1)}, u32[]{:S(2)}, u32[]{:S(2)}) %collective-permute-start.8) | collective-permute-done | bytes 262176 | tf_op jit(solution)/shard_map/ppermute | solution.py:586
  87.0 2.0 %collective-permute-start.10 = (bf16[128,1024]{1,0:T(8,128)(2,1)}, bf16[128,1024]{1,0:T(8,128)(2,1)}, u32[]{:S(2)}, u32[]{:S(2)}) collective-permute-start(bf16[128,1024]{1,0:T(8,128)(2,1)} %get-tuple-element.144), channel_id=1, source_target_pairs={{0,3},{1,2},{2,1},{3,0},{4,7},{5,6},{6,5},{7,4},{8,11},{9,10},{10,... | collective-permute-start | bytes 786440 | tf_op jit(solution)/shard_map/ppermute | solution.py:586
  89.0 1.5 wave_slots.1
  91.8 18.6 %centroid_rows.1.before = bf16[3072,1024]{1,0:T(8,128)(2,1)} custom-call(s32[3072]{0:T(1024)} %bitcast.33, s32[3072]{0:T(1024)} %fusion.2.lists, bf16[4096,1024]{1,0:T(8,128)(2,1)} %centroids.1), custom_call_target="tpu_custom_call" | custom-call | flops 1 | bytes 1 | tf_op jit(solution)/shard_map/centroid_rows/pallas_call | solution.py:475
  110.5 5.8 %collective-permute-done.7.refs_2_ = bf16[160,1024]{1,0:T(8,128)(2,1)S(1)} collective-permute-done((bf16[160,1024]{1,0:T(8,128)(2,1)}, bf16[160,1024]{1,0:T(8,128)(2,1)S(1)}, u32[]{:S(2)}, u32[]{:S(2)}) %collective-permute-start.7) | collective-permute-done | bytes 327712 | tf_op jit(solution)/shard_map/ppermute | solution.py:576
  117.0 4.0 %spread_rows.3 = (bf16[192,1024]{1,0:T(8,128)(2,1)}, bf16[192,1024]{1,0:T(8,128)(2,1)}, bf16[192,1024]{1,0:T(8,128)(2,1)}, bf16[192,1024]{1,0:T(8,128)(2,1)}) custom-call(s32[1]{0:T(128)} %bitcast.6.me, s32[8,128]{1,0:T(8,128)} %copy-done, bf16[160,1024]{1,0:T(8,128)(2,1)} %copy-done.9, bf16[160,1024]{1,0:T(8,128)(2,1)} %copy-done.10, ...), custom_call_target="tpu_custom_call" | custom-call | flops 1 | bytes 1 | tf_op jit(solution)/shard_map/spread_rows/pallas_call | solution.py:401
  122.0 1.8 collective-permute-start.13
  125.4 15.1 %residual_rows.12.before = bf16[3072,1024]{1,0:T(8,128)(2,1)} custom-call(s32[1,1536]{1,0:T(1,128)} %pad_add_fusion.slots, bf16[3072,1024]{1,0:T(8,128)(2,1)} %centroid_rows.1.before, bf16[1024,1024]{1,0:T(8,128)(2,1)} %bitcast.16.refs_0_, bf16[128,1024]{1,0:T(8,128)(2,1)} %get-tuple-element.147.refs_1_, bf16[128,1024]{1,0:T(8,128)(2,1)} %collective-permute-done.8.refs_2_, ...), custom_call_target="tpu_custom_call" | custom-call | flops 1 | bytes 1 | tf_op jit(solution)/shard_map/residual_rows/pallas_call | solution.py:522
  140.5 3.1 %collective-permute-done.3.refs_1_ = bf16[160,1024]{1,0:T(8,128)(2,1)} collective-permute-done((bf16[160,1024]{1,0:T(8,128)(2,1)}, bf16[160,1024]{1,0:T(8,128)(2,1)}, u32[]{:S(2)}, u32[]{:S(2)}) %collective-permute-start.3) | collective-permute-done | bytes 327712 | tf_op jit(solution)/shard_map/ppermute | solution.py:576
  143.6 9.1 %collective-permute-done.4.refs_2_ = bf16[160,1024]{1,0:T(8,128)(2,1)} collective-permute-done((bf16[160,1024]{1,0:T(8,128)(2,1)}, bf16[160,1024]{1,0:T(8,128)(2,1)}, u32[]{:S(2)}, u32[]{:S(2)}) %collective-permute-start.4) | collective-permute-done | bytes 327712 | tf_op jit(solution)/shard_map/ppermute | solution.py:576
  152.7 4.2 %spread_rows.2 = (bf16[192,1024]{1,0:T(8,128)(2,1)}, bf16[192,1024]{1,0:T(8,128)(2,1)}, bf16[192,1024]{1,0:T(8,128)(2,1)}, bf16[192,1024]{1,0:T(8,128)(2,1)}) custom-call(s32[1]{0:T(128)} %bitcast.6.me, s32[8,128]{1,0:T(8,128)} %copy-done, bf16[160,1024]{1,0:T(8,128)(2,1)} %collective-permute-done.2.refs_0_, ...), custom_call_target="tpu_custom_call" | custom-call | flops 1 | bytes 1 | tf_op jit(solution)/shard_map/spread_rows/pallas_call | solution.py:401
  158.0 2.5 %collective-permute-start.16 = (bf16[192,1024]{1,0:T(8,128)(2,1)}, bf16[192,1024]{1,0:T(8,128)(2,1)S(1)}, u32[]{:S(2)}, u32[]{:S(2)}) collective-permute-start(bf16[192,1024]{1,0:T(8,128)(2,1)} %get-tuple-element.174), channel_id=1, source_target_pairs={{0,3},{1,2},{2,1},{3,0},{4,7},{5,6},{6,5},{7,4},{8,11},{9,10},{10,... | collective-permute-start | bytes 1179656 | tf_op jit(solution)/shard_map/ppermute | solution.py:586
  165.9 12.3 %residual_rows.13 = bf16[3072,1024]{1,0:T(8,128)(2,1)} custom-call(s32[1,960]{1,0:T(1,128)} %pad_add_fusion.1.slots, bf16[3072,1024]{1,0:T(8,128)(2,1)} %residual_rows.12.before, bf16[192,1024]{1,0:T(8,128)(2,1)} %get-tuple-element.167.refs_0_, bf16[192,1024]{1,0:T(8,128)(2,1)} %copy-done.6, bf16[192,1024]{1,0:T(8,128)(2,1)} %copy-done.7, ...), custom_call_target="tpu_custom_call" | custom-call | flops 1 | bytes 1 | tf_op jit(solution)/shard_map/residual_rows/pallas_call | solution.py:522
  178.2 10.2 %conditional.1 = (bf16[3072,1024]{1,0:T(8,128)(2,1)}) conditional(s32[]{:T(128)} %clamp.3, (s32[1,576]{1,0:T(1,128)S(1)}, bf16[3072,1024]{1,0:T(8,128)(2,1)}, bf16[192,1024]{1,0:T(8,128)(2,1)S(1)}, bf16[192,1024]{1,0:T(8,128)(2,1)S(1)}, bf16[192,1024]{1,0:T(8,128)(2,1)S(1)}) %tuple.20, (s32[16,256]{1,0:T(8,128)S(1)}, ...), branch_computations={%region_1.2_spmd, %region_2.3_spmd, %region_3.4_spmd} | conditional | flops 16387 | bytes 18944044 | solution.py:659
  178.2 10.2 %residual_rows.7 = bf16[3072,1024]{1,0:T(8,128)(2,1)} custom-call(s32[1,576]{1,0:T(1,128)S(1)} %get-tuple-element.54.slots, bf16[3072,1024]{1,0:T(8,128)(2,1)} %get-tuple-element.56.before, bf16[192,1024]{1,0:T(8,128)(2,1)S(1)} %get-tuple-element.57.refs_0_, bf16[192,1024]{1,0:T(8,128)(2,1)S(1)} %get-tuple-element.58.refs_1_, ...), custom_call_target="tpu_custom_call" | custom-call | flops 1 | bytes 1 | tf_op jit(solution)/shard_map/cond/branch_0_fun/residual_rows/pallas_call | solution.py:522
  (81 shorter events, 23.8 us)
Async XLA Ops:
  1.3 9.9 %copy-start.1 = (s32[1024,1]{0,1:T(1,128)S(1)}, s32[1024,1]{0,1:T(1,128)}, u32[]{:S(2)}) copy-start(s32[1024,1]{0,1:T(1,128)} %param.14) | copy-start | bytes 12292
  1.3 9.9 %copy-start.2 = (s32[1024]{0:T(1024)S(1)}, s32[1024]{0:T(1024)}, u32[]{:S(2)}) copy-start(s32[1024]{0:T(1024)} %param.15) | copy-start | bytes 12292
  10.5 18.1 %collective-permute-start = (bf16[512,1280]{1,0:T(8,128)(2,1)}, bf16[512,1280]{1,0:T(8,128)(2,1)S(1)}, u32[]{:S(2)}, u32[]{:S(2)}) collective-permute-start(bf16[512,1280]{1,0:T(8,128)(2,1)} %partial_keys.5), channel_id=1, source_target_pairs={{0,16},{16,0},{1,17},{17,1},{2,18},{18,2},{3,19},{19,3},{4,20},{20... | collective-permute-start | bytes 3932168 | tf_op jit(solution)/shard_map/ppermute | solution.py:598
  13.2 21.4 %all-to-all-start.2 = ((s32[32,1,768]{2,1,0:T(1,128)}), s32[32,1,768]{2,1,0:T(1,128)S(1)}, u32[]{:S(2)}, u32[]{:S(2)}) async-start(s32[32,1,768]{2,1,0:T(1,128)} %all_to_all.21), calls=%async_computation.2 | async-start | bytes 196608 | tf_op jit(solution)/shard_map/all_to_all | solution.py:592
  34.6 90.7 %all-to-all-start.3 = ((bf16[16,64,1024]{2,1,0:T(8,128)(2,1)}), bf16[16,64,1024]{2,1,0:T(8,128)(2,1)}, u32[]{:S(2)}, u32[]{:S(2)}) async-start(bf16[16,64,1024]{2,1,0:T(8,128)(2,1)} %bitcast.31), calls=%async_computation.3 | async-start | bytes 4194304 | tf_op jit(solution)/shard_map/all_to_all | solution.py:604
  50.3 10.1 %collective-permute-start.1 = (bf16[512,1280]{1,0:T(8,128)(2,1)}, bf16[512,1280]{1,0:T(8,128)(2,1)S(1)}, u32[]{:S(2)}, u32[]{:S(2)}) collective-permute-start(bf16[512,1280]{1,0:T(8,128)(2,1)} %partial_keys.7), channel_id=1, source_target_pairs={{0,16},{16,0},{1,17},{17,1},{2,18},{18,2},{3,19},{19,3},{4,20},{20... | collective-permute-start | bytes 3932168 | tf_op jit(solution)/shard_map/ppermute | solution.py:598
  51.2 19.7 %copy-start.12 = (s32[1,3072]{1,0:T(1,128)S(1)}, s32[1,3072]{1,0:T(1,128)}, u32[]{:S(2)}) copy-start(s32[1,3072]{1,0:T(1,128)} %param.16) | copy-start | bytes 36868
  68.9 18.1 %collective-permute-start.8 = (bf16[128,1024]{1,0:T(8,128)(2,1)}, bf16[128,1024]{1,0:T(8,128)(2,1)}, u32[]{:S(2)}, u32[]{:S(2)}) collective-permute-start(bf16[128,1024]{1,0:T(8,128)(2,1)} %get-tuple-element.142), channel_id=1, source_target_pairs={{0,1},{1,0},{2,3},{3,2},{4,5},{5,4},{6,7},{7,6},{8,9},{9,8},{10,11... | collective-permute-start | bytes 786440 | tf_op jit(solution)/shard_map/ppermute | solution.py:586
  70.0 18.9 %collective-permute-start.9 = (bf16[128,1024]{1,0:T(8,128)(2,1)}, bf16[128,1024]{1,0:T(8,128)(2,1)}, u32[]{:S(2)}, u32[]{:S(2)}) collective-permute-start(bf16[128,1024]{1,0:T(8,128)(2,1)} %get-tuple-element.143), channel_id=1, source_target_pairs={{0,2},{1,3},{2,0},{3,1},{4,6},{5,7},{6,4},{7,5},{8,10},{9,11},{10,... | collective-permute-start | bytes 786440 | tf_op jit(solution)/shard_map/ppermute | solution.py:586
  72.6 37.9 %collective-permute-start.5 = (bf16[160,1024]{1,0:T(8,128)(2,1)}, bf16[160,1024]{1,0:T(8,128)(2,1)S(1)}, u32[]{:S(2)}, u32[]{:S(2)}) collective-permute-start(bf16[160,1024]{1,0:T(8,128)(2,1)} %get-tuple-element.138), channel_id=1, source_target_pairs={{0,4},{1,5},{2,6},{3,7},{4,0},{5,1},{6,2},{7,3},{8,12},{9,13},{10,... | collective-permute-start | bytes 983048 | tf_op jit(solution)/shard_map/ppermute | solution.py:576
  73.8 36.6 %collective-permute-start.6 = (bf16[160,1024]{1,0:T(8,128)(2,1)}, bf16[160,1024]{1,0:T(8,128)(2,1)S(1)}, u32[]{:S(2)}, u32[]{:S(2)}) collective-permute-start(bf16[160,1024]{1,0:T(8,128)(2,1)} %get-tuple-element.139), channel_id=1, source_target_pairs={{0,8},{1,9},{2,10},{3,11},{4,12},{5,13},{6,14},{7,15},{8,0},{9,1},... | collective-permute-start | bytes 983048 | tf_op jit(solution)/shard_map/ppermute | solution.py:576
  74.1 42.2 %collective-permute-start.7 = (bf16[160,1024]{1,0:T(8,128)(2,1)}, bf16[160,1024]{1,0:T(8,128)(2,1)S(1)}, u32[]{:S(2)}, u32[]{:S(2)}) collective-permute-start(bf16[160,1024]{1,0:T(8,128)(2,1)} %get-tuple-element.140), channel_id=1, source_target_pairs={{0,12},{1,13},{2,14},{3,15},{4,8},{5,9},{6,10},{7,11},{8,4},{9,5},... | collective-permute-start | bytes 983048 | tf_op jit(solution)/shard_map/ppermute | solution.py:576
  87.0 23.4 %collective-permute-start.10 = (bf16[128,1024]{1,0:T(8,128)(2,1)}, bf16[128,1024]{1,0:T(8,128)(2,1)}, u32[]{:S(2)}, u32[]{:S(2)}) collective-permute-start(bf16[128,1024]{1,0:T(8,128)(2,1)} %get-tuple-element.144), channel_id=1, source_target_pairs={{0,3},{1,2},{2,1},{3,0},{4,7},{5,6},{6,5},{7,4},{8,11},{9,10},{10,... | collective-permute-start | bytes 786440 | tf_op jit(solution)/shard_map/ppermute | solution.py:586
  89.0 34.8 %collective-permute-start.2 = (bf16[160,1024]{1,0:T(8,128)(2,1)}, bf16[160,1024]{1,0:T(8,128)(2,1)}, u32[]{:S(2)}, u32[]{:S(2)}) collective-permute-start(bf16[160,1024]{1,0:T(8,128)(2,1)} %get-tuple-element.133), channel_id=1, source_target_pairs={{0,4},{1,5},{2,6},{3,7},{4,0},{5,1},{6,2},{7,3},{8,12},{9,13},{10,... | collective-permute-start | bytes 983048 | tf_op jit(solution)/shard_map/ppermute | solution.py:576
  110.5 5.9 %copy-start.9 = (bf16[160,1024]{1,0:T(8,128)(2,1)}, bf16[160,1024]{1,0:T(8,128)(2,1)S(1)}, u32[]{:S(2)}) copy-start(bf16[160,1024]{1,0:T(8,128)(2,1)S(1)} %collective-permute-done.5.refs_0_) | copy-start | bytes 983044
  110.5 5.8 %copy-start.10 = (bf16[160,1024]{1,0:T(8,128)(2,1)}, bf16[160,1024]{1,0:T(8,128)(2,1)S(1)}, u32[]{:S(2)}) copy-start(bf16[160,1024]{1,0:T(8,128)(2,1)S(1)} %collective-permute-done.6.refs_1_) | copy-start | bytes 983044
  121.1 35.9 %collective-permute-start.11 = (bf16[192,1024]{1,0:T(8,128)(2,1)}, bf16[192,1024]{1,0:T(8,128)(2,1)S(1)}, u32[]{:S(2)}, u32[]{:S(2)}) collective-permute-start(bf16[192,1024]{1,0:T(8,128)(2,1)} %get-tuple-element.164), channel_id=1, source_target_pairs={{0,1},{1,0},{2,3},{3,2},{4,5},{5,4},{6,7},{7,6},{8,9},{9,8},{10,11... | collective-permute-start | bytes 1179656 | tf_op jit(solution)/shard_map/ppermute | solution.py:586
  122.0 35.0 %collective-permute-start.12 = (bf16[192,1024]{1,0:T(8,128)(2,1)}, bf16[192,1024]{1,0:T(8,128)(2,1)S(1)}, u32[]{:S(2)}, u32[]{:S(2)}) collective-permute-start(bf16[192,1024]{1,0:T(8,128)(2,1)} %get-tuple-element.165), channel_id=1, source_target_pairs={{0,2},{1,3},{2,0},{3,1},{4,6},{5,7},{6,4},{7,5},{8,10},{9,11},{10,... | collective-permute-start | bytes 1179656 | tf_op jit(solution)/shard_map/ppermute | solution.py:586
  122.0 35.0 %collective-permute-start.13 = (bf16[192,1024]{1,0:T(8,128)(2,1)}, bf16[192,1024]{1,0:T(8,128)(2,1)S(1)}, u32[]{:S(2)}, u32[]{:S(2)}) collective-permute-start(bf16[192,1024]{1,0:T(8,128)(2,1)} %get-tuple-element.166), channel_id=1, source_target_pairs={{0,3},{1,2},{2,1},{3,0},{4,7},{5,6},{6,5},{7,4},{8,11},{9,10},{10,... | collective-permute-start | bytes 1179656 | tf_op jit(solution)/shard_map/ppermute | solution.py:586
  123.7 19.9 %collective-permute-start.3 = (bf16[160,1024]{1,0:T(8,128)(2,1)}, bf16[160,1024]{1,0:T(8,128)(2,1)}, u32[]{:S(2)}, u32[]{:S(2)}) collective-permute-start(bf16[160,1024]{1,0:T(8,128)(2,1)} %get-tuple-element.134), channel_id=1, source_target_pairs={{0,8},{1,9},{2,10},{3,11},{4,12},{5,13},{6,14},{7,15},{8,0},{9,1},... | collective-permute-start | bytes 983048 | tf_op jit(solution)/shard_map/ppermute | solution.py:576
  123.7 29.0 %collective-permute-start.4 = (bf16[160,1024]{1,0:T(8,128)(2,1)}, bf16[160,1024]{1,0:T(8,128)(2,1)}, u32[]{:S(2)}, u32[]{:S(2)}) collective-permute-start(bf16[160,1024]{1,0:T(8,128)(2,1)} %get-tuple-element.135), channel_id=1, source_target_pairs={{0,12},{1,13},{2,14},{3,15},{4,8},{5,9},{6,10},{7,11},{8,4},{9,5},... | collective-permute-start | bytes 983048 | tf_op jit(solution)/shard_map/ppermute | solution.py:576
  157.9 20.3 %collective-permute-start.14 = (bf16[192,1024]{1,0:T(8,128)(2,1)}, bf16[192,1024]{1,0:T(8,128)(2,1)S(1)}, u32[]{:S(2)}, u32[]{:S(2)}) collective-permute-start(bf16[192,1024]{1,0:T(8,128)(2,1)} %get-tuple-element.172), channel_id=1, source_target_pairs={{0,1},{1,0},{2,3},{3,2},{4,5},{5,4},{6,7},{7,6},{8,9},{9,8},{10,11... | collective-permute-start | bytes 1179656 | tf_op jit(solution)/shard_map/ppermute | solution.py:586
  158.0 20.2 %collective-permute-start.15 = (bf16[192,1024]{1,0:T(8,128)(2,1)}, bf16[192,1024]{1,0:T(8,128)(2,1)S(1)}, u32[]{:S(2)}, u32[]{:S(2)}) collective-permute-start(bf16[192,1024]{1,0:T(8,128)(2,1)} %get-tuple-element.173), channel_id=1, source_target_pairs={{0,2},{1,3},{2,0},{3,1},{4,6},{5,7},{6,4},{7,5},{8,10},{9,11},{10,... | collective-permute-start | bytes 1179656 | tf_op jit(solution)/shard_map/ppermute | solution.py:586
  158.0 20.2 %collective-permute-start.16 = (bf16[192,1024]{1,0:T(8,128)(2,1)}, bf16[192,1024]{1,0:T(8,128)(2,1)S(1)}, u32[]{:S(2)}, u32[]{:S(2)}) collective-permute-start(bf16[192,1024]{1,0:T(8,128)(2,1)} %get-tuple-element.174), channel_id=1, source_target_pairs={{0,3},{1,2},{2,1},{3,0},{4,7},{5,6},{6,5},{7,4},{8,11},{9,10},{10,... | collective-permute-start | bytes 1179656 | tf_op jit(solution)/shard_map/ppermute | solution.py:586
  (7 other events, 6.1 us)
